TPU v7x, 32 devices: a whole 2x2x4 slice. The times are simulated.
32 devices in a mesh: section: 2 (over y), expert: 8 (over z, x), tensor: 2 (over core).
Axes of the slice: x: 2, y: 2, z: 4, core: 2. Of those that a mesh axis runs over, the one named last changes fastest.
Arguments:
- inputs: float32 [2, 4096, 768], P(None, ('expert', 'tensor')), may hold values from -6 to 6
- cotangent: float32 [2, 4096, 768], P(None, ('expert', 'tensor')), may hold values from -6 to 6
- prev_logits: float32 [2, 2, 4096, 12], P('section', None, ('expert', 'tensor')), may hold values from -3 to 3
- lengths: int32 [2, 8, 4], P(None, 'expert'), may hold values from 1 to 456, 512 in all within a row
- routes: int32 [2, 2, 4096, 2], P('section', None, ('expert', 'tensor')), may hold values from 0 to 11, all different within a row; in each aligned block of 256 rows (0 to 255, 256 to 511, ..., all dimensions but the last counted through in order) at most 98 rows name the same one
- slot_order: int32 [2, 2, 16, 256], P('section', None, ('expert', 'tensor')), may hold values from 0 to 255, each once within a row
- norm_gain1: float32 [2, 768], P('section'), may hold values from 0.5 to 1.5
- w_query: bfloat16 [2, 768, 768], P('section', None, 'tensor'), may hold values from -0.21875 to 0.21875
- w_key: bfloat16 [2, 768, 768], P('section', None, 'tensor'), may hold values from -0.21875 to 0.21875
- w_value: bfloat16 [2, 768, 768], P('section', None, 'tensor'), may hold values from -0.21875 to 0.21875
- w_out: bfloat16 [2, 768, 768], P('section', 'tensor'), may hold values from -0.625 to 0.625
- norm_gain2: float32 [2, 768], P('section'), may hold values from 0.5 to 1.5
- router: float32 [2, 768, 12], P('section'), may hold values from -0.109375 to 0.109375
- router_residual: float32 [2, 12, 12], P('section'), may hold values from -1.75 to 1.75
- const_gate: float32 [2, 2, 768], P('section'), may hold values from -0.21875 to 0.21875
- const_value: float32 [2, 2, 768], P('section'), may hold values from -5 to 5
- expert_gate: bfloat16 [2, 8, 768, 2048], P('section', 'expert', None, 'tensor'), may hold values from -0.21875 to 0.21875
- expert_up: bfloat16 [2, 8, 768, 2048], P('section', 'expert', None, 'tensor'), may hold values from -0.21875 to 0.21875
- expert_down: bfloat16 [2, 8, 2048, 768], P('section', 'expert', 'tensor'), may hold values from -0.125 to 0.125
Outputs:
- layer_outputs: float32 [2, 2, 4096, 768], P('section', None, ('expert', 'tensor'))
- input_grads: float32 [2, 2, 4096, 768], P('section', None, ('expert', 'tensor'))
- logit_grads: float32 [2, 2, 4096, 12], P('section', None, ('expert', 'tensor'))
- norm_gain1_grad: float32 [2, 768], P('section')
- w_query_grad: float32 [2, 768, 768], P('section', None, 'tensor')
- w_key_grad: float32 [2, 768, 768], P('section', None, 'tensor')
- w_value_grad: float32 [2, 768, 768], P('section', None, 'tensor')
- w_out_grad: float32 [2, 768, 768], P('section', 'tensor')
- norm_gain2_grad: float32 [2, 768], P('section')
- router_grad: float32 [2, 768, 12], P('section')
- router_residual_grad: float32 [2, 12, 12], P('section')
- const_gate_grad: float32 [2, 2, 768], P('section')
- const_value_grad: float32 [2, 2, 768], P('section')
- expert_gate_grad: float32 [2, 8, 768, 2048], P('section', 'expert', None, 'tensor')
- expert_up_grad: float32 [2, 8, 768, 2048], P('section', 'expert', None, 'tensor')
- expert_down_grad: float32 [2, 8, 2048, 768], P('section', 'expert', 'tensor')
Inputs may be any that keep to these rules, and one draw needn't show every extreme that they name: In each micro-batch and block, the first 3 entries are the lengths of the sequences packed in order into the block's 512 rows and the last is the number of padding rows at its end; the entries sum to 512 and the largest is exactly 456. `routes`: each row names two different choices: 0 to 7 are feed-forward experts, 8 the zero expert, 9 the copy expert, 10 and 11 the constant experts. Within the 256 rows of one device no choice is named by more than 98 rows, and every choice is named somewhere. `slot_order`: for each layer, micro-batch and device, a permutation of 0 to 256 - 1 over the device's rows.
All inputs are finite; a program needn't handle non-finite values.
Results may differ from a plain program's by a relative error of at most 0.028.
Values may be sent and summed in bfloat16 or wider, within the bound.
A program may use at most 256 MiB of HBM per device.

v0:
```python
import functools
import types

import jax
import jax.numpy as jnp
import numpy as np
from jax import lax
from jax.experimental import pallas as pl
from jax.experimental.pallas import tpu as pltpu
from jax.sharding import PartitionSpec as P

HEAD_DIM = 64
LANES = 128
EPSILON = 1e-06
MESH = pl.DeviceIdType.MESH
f32, bf16, i32 = jnp.float32, jnp.bfloat16, jnp.int32

P_NORM, P_OUT, P_ROWS, P_PART, P_GROWS, P_GPART, P_DA, P_DX = range(8)


def dot(left, right):
    return jnp.dot(left, right, preferred_element_type=f32)


def dot_nt(left, right):
    return lax.dot_general(left, right, (((1,), (1,)), ((), ())), preferred_element_type=f32)


def dot_tn(left, right):
    return lax.dot_general(left, right, (((0,), (0,)), ((), ())), preferred_element_type=f32)


def wide(values):
    return values.astype(f32)


def halves(values):
    upper = values.astype(bf16)
    return upper, (values - wide(upper)).astype(bf16)


def dot3(how, left, right):
    left_hi, left_lo = halves(left)
    right_hi, right_lo = halves(right)
    return how(left_hi, right_hi) + (how(left_hi, right_lo) + how(left_lo, right_hi))


def inverse_rms(values):
    return lax.rsqrt(jnp.mean(values * values, axis=-1, keepdims=True) + EPSILON)


def iota(shape, dim):
    return lax.broadcasted_iota(i32, shape, dim)


def flag(condition):
    return wide(condition.astype(i32))


def half_lanes(width):
    return (iota((1, width), 1) % HEAD_DIM) < HEAD_DIM // 2


def turned(values, cosine, sine):
    quarter = HEAD_DIM // 2
    other = jnp.where(
        half_lanes(LANES),
        -pltpu.roll(values, LANES - quarter, 1),
        pltpu.roll(values, quarter, 1),
    )
    return values * cosine + other * sine


def turned_back(values, cosine, sine):
    quarter = HEAD_DIM // 2
    other = jnp.where(
        half_lanes(LANES),
        pltpu.roll(values, LANES - quarter, 1),
        -pltpu.roll(values, quarter, 1),
    )
    return values * cosine + other * sine


def chain_kernel(cfg, names, *refs):
    r = types.SimpleNamespace(**dict(zip(names, refs, strict=True)))
    owned, rows, experts, cap, slots = cfg.owned, cfg.rows, cfg.experts, cfg.cap, cfg.slots
    choices, micro, sections, seqs = cfg.choices, cfg.micro, cfg.sections, cfg.seqs
    pairs, chunk = cfg.heads // 2, cfg.chunk
    scale = HEAD_DIM ** (-0.5)
    sec, me, core = (lax.axis_index(a) for a in ("section", "expert", "tensor"))
    other = 1 - core
    own_rows = pl.ds(pl.multiple_of(core * owned, owned), owned)
    other_rows = pl.ds(pl.multiple_of(other * owned, owned), owned)
    is_first, is_last = sec == 0, sec == sections - 1

    deep = cfg.depth == micro

    def slot(m):
        return m if deep else 0

    def pair(kind, m, j, source, target):
        return pltpu.make_async_remote_copy(
            src_ref=source,
            dst_ref=target,
            send_sem=r.pair_send.at[kind, m, j],
            recv_sem=r.pair_recv.at[kind, m, j],
            device_id={"tensor": other},
            device_id_type=MESH,
        )

    def hop(kind, m, source, target, section):
        return pltpu.make_async_remote_copy(
            src_ref=source,
            dst_ref=target,
            send_sem=r.hop_send.at[kind, m],
            recv_sem=r.hop_recv.at[kind, m],
            device_id={"section": section},
            device_id_type=MESH,
        )

    main, rem, half_rows, rem_rows = cfg.main, cfg.rem, cfg.half_rows, cfg.rem_rows
    rem_start = experts * main
    group = experts // 2
    my_group, in_group = me // group, lax.rem(me, group)
    group_of = (my_group, 1 - my_group)

    def slot_rows(index):
        return pl.ds(pl.multiple_of(index * main, main), main)

    def group_rows(g, offset=0):
        return pl.ds(pl.multiple_of(offset + group_of[g] * half_rows, 16), half_rows)

    def last_rows(offset=0):
        return pl.ds(pl.multiple_of(offset + rem_start, 16), rem_rows)

    def get(ref, g, offset=0, cols=slice(None)):
        value = ref[group_rows(g, offset), cols]
        if g == 1 and rem:
            value = jnp.concatenate([value, ref[last_rows(offset), cols]], axis=0)
        return value

    def put(ref, g, value, offset=0, cols=slice(None)):
        ref[group_rows(g, offset), cols] = value[:half_rows]
        if g == 1 and rem:
            ref[last_rows(offset), cols] = value[half_rows:]

    pieces = -(-half_rows // 256)
    hidden_cols = [
        slice(k * cfg.inner // pieces, (k + 1) * cfg.inner // pieces) for k in range(pieces)
    ]

    def parts(g):
        return [group_rows(g)] + ([last_rows()] if g == 1 and rem else [])

    def peers_in(g, act):
        def step(k, carry):
            act(group_of[g] * group + lax.rem(in_group + k, group))
            return carry

        lax.fori_loop(1 - g, group, step, 0)

    def exchange(kind, m, peer, landed, source, target):
        return pltpu.make_async_remote_copy(
            src_ref=source.at[slot_rows(peer)],
            dst_ref=target.at[slot_rows(landed)],
            send_sem=r.a2a_send.at[kind, m, peer],
            recv_sem=r.a2a_recv.at[kind, m, landed],
            device_id={"expert": peer},
            device_id_type=MESH,
        )

    def exchange_rem(kind, m, peer, landed, source, target):
        return pltpu.make_async_remote_copy(
            src_ref=source.at[peer],
            dst_ref=target.at[landed],
            send_sem=r.rem_send.at[kind, m, peer],
            recv_sem=r.rem_recv.at[kind, m, landed],
            device_id={"expert": peer},
            device_id_type=MESH,
        )

    def lay_rem(ref, value):
        for k in range(rem):
            ref[:, k, :] = value[k * experts : (k + 1) * experts]

    def read_rem(ref):
        value = [ref[:, k, :] for k in range(rem)]
        rest = rem_rows - rem * experts
        if rest:
            value.append(jnp.zeros((rest, cfg.width), f32))
        return jnp.concatenate(value, axis=0).astype(bf16)

    def send_slots(kind, m, value):
        d = slot(m)
        outgoing, mine = r.outgoing.at[d], r.arrived.at[d, core]
        r.outgoing[d] = value[:rem_start].astype(bf16)
        for g in (1, 0):
            peers_in(g, lambda p: exchange(kind, m, p, me, outgoing, mine).start())
        if rem:
            rem_out, rem_in = r.rem_out.at[d], r.rem_in.at[d]
            lay_rem(rem_out, value[rem_start:])
            for g in (1, 0):
                peers_in(g, lambda p: exchange_rem(kind, m, p, me, rem_out, rem_in).start())
            rem_in[pl.ds(me, 1)] = rem_out[pl.ds(me, 1)]
        mine[slot_rows(me), :] = outgoing[slot_rows(me), :]

    def save(index, m, source, target):
        return pltpu.make_async_copy(source, target.at[m], r.local.at[index, m])

    def grad_back(m):
        return r.inside.at[slot(m), pl.ds(0, slots), pl.ds(0, cfg.width)]

    back_hop = min(1, sections - 2)
    def stage(m):
        return r.stage.at[m] if deep else r.partial.at[pl.ds(0, owned)]


    barrier = pltpu.get_barrier_semaphore()

    def greet(k, carry):
        pl.semaphore_signal(
            barrier, inc=1, device_id={"expert": lax.rem(me + k, experts)}, device_id_type=MESH
        )
        return carry

    lax.fori_loop(1, experts, greet, 0)
    pl.semaphore_signal(barrier, inc=1, device_id={"tensor": other}, device_id_type=MESH)

    @pl.when(sec > 0)
    def _():
        pl.semaphore_signal(barrier, inc=1, device_id={"section": sec - 1}, device_id_type=MESH)

    @pl.when(sec < sections - 1)
    def _():
        pl.semaphore_signal(barrier, inc=1, device_id={"section": sec + 1}, device_id_type=MESH)

    for m in range(micro):

        @pl.when(is_first)
        def _():
            pltpu.make_async_copy(r.inputs.at[m], r.x.at[m], r.local.at[0, m]).start()

        if deep:

            @pl.when(is_last)
            def _():
                pltpu.make_async_copy(r.cotangent.at[m], r.dz.at[m], r.local.at[9, m]).start()

    weights = [
        pltpu.make_async_copy(source, target, r.fetch.at[k])
        for k, (source, target) in enumerate(
            ((r.gate, r.gate_v), (r.up, r.up_v), (r.down, r.down_v))
        )
    ]
    for copy in weights:
        copy.start()
    beside = (sec > 0).astype(i32) + (sec < sections - 1).astype(i32)
    pl.semaphore_wait(barrier, experts + beside)

    r.mixer[...] = jnp.zeros_like(r.mixer)
    r.mixer[:choices, :] = r.router_in[...]
    r.mixer[choices : choices + 2, :] = r.const_gate[...]
    r.residual[...] = jnp.zeros_like(r.residual)
    r.residual[:choices, :choices] = r.residual_in[...]
    r.prev_t[...] = jnp.zeros_like(r.prev_t)
    for m in range(micro):
        r.prev_t[m, :choices, :] = r.prev_in[:, m, :]
        table = jnp.concatenate(
            [r.route_row[m], r.order_row[m], jnp.zeros((13, owned), i32)], axis=0
        )
        unit = flag(iota((owned, owned), 0) == iota((owned, owned), 1)).astype(bf16)
        r.cols[m] = dot_nt(unit, wide(table).astype(bf16)).astype(i32)

    def seq_bias(m):
        row = iota((rows, 1), 0)
        start = jnp.zeros((rows, 1), i32)
        end = r.lengths[m, 0]
        for k in range(seqs):
            start = jnp.where(row >= end, row if k == seqs - 1 else end, start)
            end = end + r.lengths[m, min(k + 1, seqs)]
        for c in range(rows // chunk):
            piece = slice(c * chunk, (c + 1) * chunk)
            key = iota((chunk, rows), 1)
            seen = (key <= row[piece]) & (key >= start[piece])
            r.bias[piece, :] = jnp.where(seen, 0.0, -1e30).astype(bf16)

    def routing(m):
        lane = iota((owned, LANES), 1)
        lane_t = iota((LANES, owned), 0)
        col = [r.cols[m, :, k : k + 1] for k in range(2)]
        row = [r.route_row[m, k : k + 1, :] for k in range(2)]
        order_row, order_col = r.order_row[m], r.cols[m, :, 2:3]
        hot = [wide((lane == col[k]).astype(i32)) for k in range(2)]
        hot_t = [wide((lane_t == row[k]).astype(i32)) for k in range(2)]
        before = wide((order_row < order_col).astype(i32)).astype(bf16)
        before_t = wide((order_col < order_row).astype(i32)).astype(bf16)
        earlier = dot(before, (hot[0] + hot[1]).astype(bf16))
        earlier_t = dot((hot_t[0] + hot_t[1]).astype(bf16), before_t)
        for k in range(2):
            slot = jnp.sum(earlier * hot[k], axis=1, keepdims=True).astype(i32)
            slot_t = jnp.sum(earlier_t * hot_t[k], axis=0, keepdims=True).astype(i32)

            def placed(choice, at):
                first = choice * main + at
                late = rem_start + (at - main) * experts + choice
                kept = (choice < experts) & (at < cap)
                return jnp.where(kept, jnp.where(at < main, first, late), -1)

            place, place_t = placed(col[k], slot), placed(row[k], slot_t)
            r.place_col[m, :, k : k + 1] = place
            r.place_row[m, k : k + 1, :] = place_t

    def spread(m, k):
        return flag(iota((owned, slots), 1) == r.place_col[m, :, k : k + 1]).astype(bf16)

    def spread_t(m, k):
        return flag(iota((slots, owned), 0) == r.place_row[m, k : k + 1, :]).astype(bf16)

    def choice_flags(m):
        col = [r.cols[m, :, k : k + 1] for k in range(2)]
        copies = [wide((col[k] == experts + 1).astype(i32)) for k in range(2)]
        consts = [
            [wide((col[k] == experts + 2 + c).astype(i32)) for c in range(2)] for k in range(2)
        ]
        return col, copies, consts

    def unpack_gates(m):
        pack = r.gates[m]
        return [pack[:, k : k + 1] for k in range(2)], [pack[:, 2 + k : 3 + k] for k in range(2)]

    def through_expert(m, kind, pair_in, pair_out, target, kept, compute):
        d = slot(m)
        arrived, outgoing, result = r.arrived.at[d], r.outgoing.at[d], r.result.at[d]
        mine, theirs = arrived.at[core], arrived.at[other]
        if rem:
            rem_out, rem_in = r.rem_out.at[d], r.rem_in.at[d]
            rem_result, rem_back = r.rem_result.at[d], r.rem_back.at[d]
        passes = kind // 2

        def keep(index, half, rows_of):
            return pltpu.make_async_copy(
                arrived.at[half, rows_of], kept.at[m, half, rows_of], r.keep.at[passes, m, index]
            )

        def forward_pair(g, which, side):
            return [
                pair(pair_in, m, g + k, side.at[rows_of], side.at[rows_of])
                for k, rows_of in enumerate(parts(g))
            ]

        def sums(g):
            return [
                pair(pair_out, m, g + k, r.part_out.at[rows_of], r.part_in.at[rows_of])
                for k, rows_of in enumerate(parts(g))
            ]

        everything = pl.ds(0, slots)

        def kept_mine(g):
            return [keep(2 * g + k, core, rows_of) for k, rows_of in enumerate(parts(g))]

        def arrive(g):
            peers_in(g, lambda p: exchange(kind, m, p, p, outgoing, mine).wait_recv())
            if g == 1 and rem:
                for which in range(2):
                    peers_in(which, lambda p: exchange_rem(kind, m, p, p, rem_out, rem_in).wait_recv())
                mine[last_rows(), :] = read_rem(rem_in)
            for copy in forward_pair(g, core, mine):
                copy.start()
            for copy in kept_mine(g):
                copy.start()

        def work(g):
            put(r.partial, g, compute(core, g))
            for copy in forward_pair(g, other, theirs):
                copy.wait_recv()
            if g == 1:
                keep(1, other, everything).start()
            put(r.part_out, g, compute(other, g).astype(bf16))
            if g == 1:
                keep(1, other, everything).wait()
            for copy in sums(g):
                copy.start()

        def finish(g):
            for copy in sums(g):
                copy.wait_recv()
            value = get(r.partial, g) + wide(get(r.part_in, g))
            for copy in kept_mine(g):
                copy.wait()
            for copy in forward_pair(g, core, mine):
                copy.wait_send()
            put(result, g, value.astype(bf16))
            peers_in(g, lambda p: exchange(kind + 1, m, p, me, result, target).start())
            if g == 1 and rem:
                lay_rem(rem_result, value[half_rows:])
                for which in (1, 0):
                    peers_in(
                        which,
                        lambda p: exchange_rem(kind + 1, m, p, me, rem_result, rem_back).start(),
                    )
                rem_back[pl.ds(me, 1)] = rem_result[pl.ds(me, 1)]

        arrive(0)
        work(0)
        arrive(1)
        finish(0)
        work(1)
        finish(1)
        target[slot_rows(me), :] = result[slot_rows(me), :]
        for g in range(2):
            for copy in sums(g):
                copy.wait_send()
            peers_in(g, lambda p: exchange(kind, m, p, me, outgoing, mine).wait_send())
            if rem:
                peers_in(g, lambda p: exchange_rem(kind, m, p, me, rem_out, rem_in).wait_send())

    def wait_back(m, kind, target):
        result = r.result.at[slot(m)]
        if rem:
            rem_result, rem_back = r.rem_result.at[slot(m)], r.rem_back.at[slot(m)]
        for g in range(2):
            peers_in(g, lambda p: exchange(kind + 1, m, p, p, result, target).wait_recv())
            if rem:
                peers_in(g, lambda p: exchange_rem(kind + 1, m, p, p, rem_result, rem_back).wait_recv())
        if rem:
            target[last_rows(), :] = read_rem(rem_back)
        for g in range(2):
            peers_in(g, lambda p: exchange(kind + 1, m, p, me, result, target).wait_send())
            if rem:
                peers_in(g, lambda p: exchange_rem(kind + 1, m, p, me, rem_result, rem_back).wait_send())

    def attend(m):
        @pl.when(is_first)
        def _():
            pltpu.make_async_copy(r.inputs.at[m], r.x.at[m], r.local.at[0, m]).wait()

        @pl.when(sec > 0)
        def _():
            hop(0, m, r.hop_out.at[slot(m)], r.hop_in.at[0, m], sec - 1).wait_recv()
            r.x[m] = wide(r.hop_in[0, m])

        x = r.x[m]
        r.norm[m, own_rows, :] = (x * inverse_rms(x) * r.gain1[...]).astype(bf16)
        pair(P_NORM, m, 0, r.norm.at[m, own_rows], r.norm.at[m, own_rows]).start()
        routing(m)
        seq_bias(m)

        def project(some):
            normed = r.norm[m, some, :]
            cosine, sine = r.cosine[some, :], r.sine[some, :]
            for stash, weight in ((r.q, r.w_query), (r.k, r.w_key)):
                flat = dot(normed, weight[...])
                for p in range(pairs):
                    lanes = slice(p * LANES, (p + 1) * LANES)
                    stash[m, some, lanes] = turned(flat[:, lanes], cosine, sine).astype(bf16)
            r.v[m, some, :] = dot(normed, r.w_value[...]).astype(bf16)

        project(own_rows)
        pair(P_NORM, m, 0, r.norm.at[m, other_rows], r.norm.at[m, other_rows]).wait_recv()
        save(1, m, r.norm.at[m], r.h_norm).start()
        project(other_rows)

        r.logsum[m] = jnp.zeros((rows, LANES), f32)
        lane = iota((1, LANES), 1)

        def head_pair(p, inner):
            lanes = pl.ds(pl.multiple_of(p * LANES, LANES), LANES)
            q2, k2, v2 = r.q[m, :, lanes], r.k[m, :, lanes], r.v[m, :, lanes]
            for half in range(2):
                keep = wide(((lane // HEAD_DIM) == half).astype(i32)).astype(bf16)
                km, vm = k2 * keep, v2 * keep
                for c in range(rows // chunk):
                    piece, reach = slice(c * chunk, (c + 1) * chunk), (c + 1) * chunk
                    scores = dot_nt(q2[piece], km[:reach]) * scale + wide(r.bias[piece, :reach])
                    peak = jnp.max(scores, axis=-1, keepdims=True)
                    shifted = jnp.exp(scores - peak)
                    total = jnp.sum(shifted, axis=-1, keepdims=True)
                    probs = (shifted * (1.0 / total)).astype(bf16)
                    mixed = dot(probs, vm[:reach])
                    if half == 0:
                        r.mix[piece, :] = mixed
                    else:
                        r.o[m, piece, lanes] = (r.mix[piece, :] + mixed).astype(bf16)
                    r.logsum[m, piece, :] = jnp.where(
                        lane == 2 * p + half, peak + jnp.log(total), r.logsum[m, piece, :]
                    )
            return inner

        lax.fori_loop(0, pairs, head_pair, 0)
        save(2, m, r.o.at[m], r.h_o).start()

    def attend_send(m):
        r.half_out[...] = dot(r.o[m, other_rows, :], r.w_out[...]).astype(bf16)
        pair(P_OUT, m, 0, r.half_out, r.half_in.at[0, m]).start()
        summed = r.x[m] + dot(r.o[m, own_rows, :], r.w_out[...])
        pair(P_OUT, m, 0, r.half_out, r.half_in.at[0, m]).wait_recv()
        hidden = summed + wide(r.half_in[0, m])
        r.h[m] = hidden
        normed2 = (hidden * inverse_rms(hidden) * r.gain2[...]).astype(bf16)
        r.norm2[m] = normed2

        send_slots(0, m, dot(spread_t(m, 0) + spread_t(m, 1), normed2))

        mixer_hi, mixer_lo = halves(r.mixer[...])
        logits = dot_nt(normed2, mixer_hi) + dot_nt(normed2, mixer_lo)
        logits = logits + dot3(dot_tn, r.prev_t[m], r.residual[...])
        col, copies, consts = choice_flags(m)
        wide_lane = iota((owned, LANES), 1)
        picked = [
            jnp.sum(jnp.where(wide_lane == col[k], logits, 0.0), axis=1, keepdims=True)
            for k in range(2)
        ]
        gate = [jax.nn.sigmoid(picked[0] - picked[1]), jax.nn.sigmoid(picked[1] - picked[0])]
        rate = [jax.nn.sigmoid(logits[:, choices + c : choices + c + 1]) for c in range(2)]
        pack = jnp.zeros((owned, LANES), f32)
        for k, value in enumerate(gate + rate):
            pack = jnp.where(wide_lane == k, value, pack)
        r.gates[m] = pack
        pair(P_NORM, m, 0, r.norm.at[m, own_rows], r.norm.at[m, own_rows]).wait_send()
        pair(P_OUT, m, 0, r.half_out, r.half_in.at[0, m]).wait_send()

    def kept_forward(m):
        copies = [save(10, m, r.inside.at[slot(m)], r.h_inside)]
        if not deep:
            copies += [
                save(5, m, r.by_up.at[0], r.h_up),
                save(6, m, r.by_gate.at[0], r.h_gate),
            ]
        return copies

    def experts_forward(m):
        d = slot(m)
        by_up, by_gate, inside_of, arrived = r.by_up.at[d], r.by_gate.at[d], r.inside.at[d], r.arrived.at[d]

        @pl.when(m == 0)
        def _():
            for copy in weights:
                copy.wait()

        def compute(half, g):
            block = get(arrived.at[half], g)
            offset = half * slots
            total = 0.0
            for cols in hidden_cols:
                value = dot(block, r.gate_v[:, cols])
                upper = dot(block, r.up_v[:, cols])
                sig = jax.nn.sigmoid(value)
                active = value * sig
                inside = (active * upper).astype(bf16)
                put(by_up, g, active.astype(bf16), offset, cols)
                slope = upper * sig * (1.0 + value * (1.0 - sig))
                put(by_gate, g, slope.astype(bf16), offset, cols)
                put(inside_of, g, inside, offset, cols)
                total = total + dot(inside, r.down_v[cols, :])
            return total

        through_expert(m, 0, P_ROWS, P_PART, r.back.at[m], r.h_rows, compute)
        for copy in kept_forward(m):
            copy.start()

    def combine(m):
        gate, rate = unpack_gates(m)
        col, copies, consts = choice_flags(m)
        wait_back(m, 0, r.back.at[m])

        apart = [dot(spread(m, k), r.back[m]) for k in range(2)]
        out = r.h[m] + gate[0] * apart[0] + gate[1] * apart[1]
        own = gate[0] * copies[0] + gate[1] * copies[1]
        for c in range(2):
            on = gate[0] * consts[0][c] + gate[1] * consts[1][c]
            own = own + on * rate[c]
            out = out + (on * (1.0 - rate[c])) * r.const_value[c : c + 1, :]
        out = out + own * wide(r.norm2[m])
        stage(m)[...] = out
        save(3, m, stage(m), r.layer_out).start()

        @pl.when(sec < sections - 1)
        def _():
            r.hop_out[slot(m)] = out.astype(bf16)
            hop(0, m, r.hop_out.at[slot(m)], r.hop_in.at[0, m], sec + 1).start()

    def settle_forward(m):
        @pl.when(sec < sections - 1)
        def _():
            hop(0, m, r.hop_out.at[slot(m)], r.hop_in.at[0, m], sec + 1).wait_send()

        save(3, m, stage(m), r.layer_out).wait()
        save(1, m, r.norm.at[m], r.h_norm).wait()
        save(2, m, r.o.at[m], r.h_o).wait()
        for copy in kept_forward(m):
            copy.wait()

    r.mixer_grad[...] = jnp.zeros_like(r.mixer_grad)
    r.residual_grad[...] = jnp.zeros_like(r.residual_grad)
    r.rows_grad[...] = jnp.zeros_like(r.rows_grad)

    def fetched(m):
        return [
            pltpu.make_async_copy(r.h_up.at[m], r.by_up.at[0], r.local.at[7, m]),
            pltpu.make_async_copy(r.h_gate.at[m], r.by_gate.at[0], r.local.at[8, m]),
        ]

    def grad_start(m):
        d = slot(m)
        if deep:
            settle_forward(m)
        else:
            for copy in fetched(m):
                copy.start()

        @pl.when(is_last)
        def _():
            copy = pltpu.make_async_copy(r.cotangent.at[m], r.dz.at[d], r.local.at[9, m])
            if not deep:
                copy.start()
            copy.wait()

        @pl.when(sec < sections - 1)
        def _():
            hop(1, m, r.hop_out.at[d], r.hop_in.at[back_hop, m], sec + 1).wait_recv()
            r.dz[d] = wide(r.hop_in[back_hop, m])

        dz = r.dz[d]
        gate, rate = unpack_gates(m)
        leaving = [dot(spread_t(m, k), (gate[k] * dz).astype(bf16)) for k in range(2)]
        send_slots(2, m, leaving[0] + leaving[1])

        col, copies, consts = choice_flags(m)
        normed2 = r.norm2[m]
        dz_norm = jnp.sum(dz * wide(normed2), axis=1, keepdims=True)
        dz_const = [
            jnp.sum(dz * r.const_value[c : c + 1, :], axis=1, keepdims=True) for c in range(2)
        ]
        apart = [dot(spread(m, k), r.back[m]) for k in range(2)]
        dgate = []
        for k in range(2):
            value = jnp.sum(dz * apart[k], axis=1, keepdims=True)
            value = value + copies[k] * dz_norm
            for c in range(2):
                value = value + consts[k][c] * (rate[c] * dz_norm + (1.0 - rate[c]) * dz_const[c])
            dgate.append(value)
        coupled = gate[0] * gate[1] * (dgate[0] - dgate[1])
        lane = iota((owned, LANES), 1)
        dlogits = jnp.where(lane == col[0], coupled, jnp.where(lane == col[1], -coupled, 0.0))
        own = gate[0] * copies[0] + gate[1] * copies[1]
        for c in range(2):
            on = gate[0] * consts[0][c] + gate[1] * consts[1][c]
            own = own + on * rate[c]
            dmix = on * (dz_norm - dz_const[c]) * rate[c] * (1.0 - rate[c])
            dlogits = dlogits + jnp.where(lane == choices + c, dmix, 0.0)
            r.rows_grad[c : c + 1, :] += jnp.sum((on * (1.0 - rate[c])) * dz, axis=0, keepdims=True)
        dlogits_hi, dlogits_lo = halves(dlogits)
        r.mixer_grad[...] += dot_tn(dlogits_hi, normed2) + dot_tn(dlogits_lo, normed2)
        r.residual_grad[...] += dot3(dot, r.prev_t[m], dlogits)
        r.logit_grad[m] = dot3(dot_nt, dlogits, r.residual[...])
        r.dnorm[d] = dot3(dot, dlogits, r.mixer[...]) + own * dz

    def kept_backward(m):
        return [
            save(11, m, r.by_up.at[slot(m)], r.h_up),
            save(12, m, r.by_gate.at[slot(m)], r.h_gate),
        ]

    def experts_backward(m):
        d = slot(m)
        by_up, by_gate, arrived = r.by_up.at[d], r.by_gate.at[d], r.arrived.at[d]
        if not deep:
            for copy in fetched(m):
                copy.wait()

        def compute(half, g):
            block = get(arrived.at[half], g)
            offset = half * slots
            total = 0.0
            for cols in hidden_cols:
                dinside = dot_nt(block, r.down_v[cols, :])
                dvalue = (dinside * wide(get(by_gate, g, offset, cols))).astype(bf16)
                dupper = (dinside * wide(get(by_up, g, offset, cols))).astype(bf16)
                put(by_gate, g, dvalue, offset, cols)
                put(by_up, g, dupper, offset, cols)
                total = total + dot_nt(dvalue, r.gate_v[:, cols]) + dot_nt(dupper, r.up_v[:, cols])
            return total

        through_expert(m, 2, P_GROWS, P_GPART, grad_back(m), r.h_grads, compute)
        for copy in kept_backward(m):
            copy.start()

    def grad_attend(m):
        d = slot(m)
        wait_back(m, 2, grad_back(m))

        both = spread(m, 0) + spread(m, 1)
        dnorm = r.dnorm[d] + dot(both, grad_back(m)[...])
        hidden = r.h[m]
        root = inverse_rms(hidden)
        scaled = dnorm * r.gain2[...]
        pull = root * root * root * jnp.mean(hidden * scaled, axis=-1, keepdims=True)
        dhidden = r.dz[d] + root * scaled - hidden * pull
        r.rows_grad[3:4, :] += jnp.sum(dnorm * hidden * root, axis=0, keepdims=True)
        r.dh[...] = dhidden
        r.da[own_rows, :] = dhidden.astype(bf16)
        pair(P_DA, m, 0, r.da.at[own_rows], r.da.at[own_rows]).start()
        seq_bias(m)
        r.do[own_rows, :] = dot_nt(r.da[own_rows, :], r.w_out[...]).astype(bf16)
        pair(P_DA, m, 0, r.da.at[other_rows], r.da.at[other_rows]).wait_recv()
        save(13, m, r.da, r.h_da).start()
        r.do[other_rows, :] = dot_nt(r.da[other_rows, :], r.w_out[...]).astype(bf16)

        head_lane = iota((1, LANES), 1)

        def head_pair(p, inner):
            lanes = pl.ds(pl.multiple_of(p * LANES, LANES), LANES)
            q2, k2, v2 = r.q[m, :, lanes], r.k[m, :, lanes], r.v[m, :, lanes]
            do2 = r.do[:, lanes]
            for half in range(2):
                keep = wide(((head_lane // HEAD_DIM) == half).astype(i32)).astype(bf16)
                km, vm, qm, dom = k2 * keep, v2 * keep, q2 * keep, do2 * keep
                for c in range(rows // chunk):
                    piece, reach = slice(c * chunk, (c + 1) * chunk), (c + 1) * chunk
                    scores = dot_nt(q2[piece], km[:reach]) * scale + wide(r.bias[piece, :reach])
                    total = jnp.sum(
                        jnp.where(head_lane == 2 * p + half, r.logsum[m, piece, :], 0.0),
                        axis=1,
                        keepdims=True,
                    )
                    probs = jnp.exp(scores - total)
                    dprobs = dot_nt(do2[piece], vm[:reach])
                    meant = jnp.sum(dprobs * probs, axis=-1, keepdims=True)
                    dscores = (probs * (dprobs - meant)).astype(bf16)
                    dq = dot(dscores, km[:reach])
                    dk = dot_tn(dscores, qm[piece])
                    dv = dot_tn(probs.astype(bf16), dom[piece])
                    if half == 0:
                        r.mix[piece, :] = dq
                    else:
                        r.mix[piece, :] += dq
                    if half == 0 and c == 0:
                        r.mix_k[...] = jnp.zeros_like(r.mix_k)
                        r.mix_v[...] = jnp.zeros_like(r.mix_v)
                    r.mix_k[:reach, :] += dk
                    r.mix_v[:reach, :] += dv
            r.dq[:, lanes] = (turned_back(r.mix[...], r.cosine[...], r.sine[...]) * scale).astype(bf16)
            r.dk[:, lanes] = (turned_back(r.mix_k[...], r.cosine[...], r.sine[...]) * scale).astype(bf16)
            r.dv[:, lanes] = r.mix_v[...].astype(bf16)
            return inner

        lax.fori_loop(0, pairs, head_pair, 0)
        for copy in kept_heads(m):
            copy.start()

    def kept_heads(m):
        return [save(14, m, r.dq, r.h_dq), save(15, m, r.dk, r.h_dk), save(16, m, r.dv, r.h_dv)]

    def grad_finish(m):
        d = slot(m)

        def dnormed(piece):
            return (
                dot_nt(r.dq[piece, :], r.w_query[...])
                + dot_nt(r.dk[piece, :], r.w_key[...])
                + dot_nt(r.dv[piece, :], r.w_value[...])
            )

        save(13, m, r.da, r.h_da).wait()
        r.half_out[...] = dnormed(other_rows).astype(bf16)
        pair(P_DX, m, 0, r.half_out, r.half_in.at[1, m]).start()
        kept = dnormed(own_rows)
        pair(P_DX, m, 0, r.half_out, r.half_in.at[1, m]).wait_recv()
        dnorm1 = kept + wide(r.half_in[1, m])
        x = r.x[m]
        root1 = inverse_rms(x)
        scaled1 = dnorm1 * r.gain1[...]
        pull1 = root1 * root1 * root1 * jnp.mean(x * scaled1, axis=-1, keepdims=True)
        dx = r.dh[...] + root1 * scaled1 - x * pull1
        stage(m)[...] = dx
        save(4, m, stage(m), r.input_grad).start()

        @pl.when(sec > 0)
        def _():
            r.hop_out[d] = dx.astype(bf16)
            hop(1, m, r.hop_out.at[d], r.hop_in.at[back_hop, m], sec - 1).start()

        r.rows_grad[2:3, :] += jnp.sum(dnorm1 * x * root1, axis=0, keepdims=True)
        pair(P_DA, m, 0, r.da.at[own_rows], r.da.at[own_rows]).wait_send()
        pair(P_DX, m, 0, r.half_out, r.half_in.at[1, m]).wait_send()
        for copy in kept_heads(m):
            copy.wait()

    def settle_backward(m):
        @pl.when(sec > 0)
        def _():
            hop(1, m, r.hop_out.at[slot(m)], r.hop_in.at[back_hop, m], sec - 1).wait_send()

        save(4, m, stage(m), r.input_grad).wait()
        for copy in kept_backward(m):
            copy.wait()

    if deep:
        def all_of(*phases):
            def step(m, carry):
                for phase in phases:
                    phase(m)
                return carry

            lax.fori_loop(0, micro, step, 0)

        def turn(m):
            combine(m)

            @pl.when(is_last)
            def _():
                grad_start(m)

        def start_rest(m):
            @pl.when(sec < sections - 1)
            def _():
                grad_start(m)

        all_of(attend, attend_send)
        all_of(experts_forward)
        all_of(turn)
        all_of(start_rest)
        all_of(experts_backward)
        all_of(grad_attend, grad_finish)
        for m in range(micro):
            settle_backward(m)
    else:

        def there(m, carry):
            for phase in (attend, attend_send, experts_forward, combine, settle_forward):
                phase(m)
            return carry

        def back_again(m, carry):
            for phase in (grad_start, experts_backward, grad_attend, grad_finish, settle_backward):
                phase(m)
            return carry

        lax.fori_loop(0, micro, there, 0)
        lax.fori_loop(0, micro, back_again, 0)


def run_chain(cfg, ins):
    vmem, anywhere = pl.BlockSpec(memory_space=pltpu.VMEM), pl.BlockSpec(memory_space=pl.ANY)
    smem = pl.BlockSpec(memory_space=pltpu.SMEM)
    far = {"inputs", "cotangent", "gate", "up", "down"}
    micro, owned, rows, width, inner = cfg.micro, cfg.owned, cfg.rows, cfg.width, cfg.inner
    heads_width, slots = cfg.heads * HEAD_DIM, cfg.slots
    shape = jax.ShapeDtypeStruct
    outs = dict(
        logit_grad=shape((micro, owned, LANES), f32),
        mixer_grad=shape((LANES, width), f32),
        residual_grad=shape((LANES, LANES), f32),
        rows_grad=shape((8, width), f32),
    )
    hbm_outs = dict(
        layer_out=shape((micro, owned, width), f32),
        input_grad=shape((micro, owned, width), f32),
        h_rows=shape((micro, 2, slots, width), bf16),
        h_grads=shape((micro, 2, slots, width), bf16),
        h_inside=shape((micro, 2 * slots, inner), bf16),
        h_up=shape((micro, 2 * slots, inner), bf16),
        h_gate=shape((micro, 2 * slots, inner), bf16),
        h_norm=shape((micro, rows, width), bf16),
        h_da=shape((micro, rows, width), bf16),
        h_o=shape((micro, rows, heads_width), bf16),
        h_dq=shape((micro, rows, heads_width), bf16),
        h_dk=shape((micro, rows, heads_width), bf16),
        h_dv=shape((micro, rows, heads_width), bf16),
    )
    dma = pltpu.SemaphoreType.DMA
    depth = cfg.depth
    rem_scratch = {}
    if depth == micro:
        rem_scratch = dict(stage=pltpu.VMEM((micro, owned, width), f32))
    if cfg.rem:
        last = pltpu.VMEM((depth, cfg.experts, cfg.rem, width), f32)
        rem_sem = dma((4, micro, cfg.experts))
        rem_scratch |= dict(
            rem_out=last, rem_in=last, rem_result=last, rem_back=last, rem_send=rem_sem, rem_recv=rem_sem
        )
    scratch = dict(
        gate_v=pltpu.VMEM((width, inner), bf16),
        up_v=pltpu.VMEM((width, inner), bf16),
        down_v=pltpu.VMEM((inner, width), bf16),
        x=pltpu.VMEM((micro, owned, width), f32),
        h=pltpu.VMEM((micro, owned, width), f32),
        norm=pltpu.VMEM((micro, rows, width), bf16),
        norm2=pltpu.VMEM((micro, owned, width), bf16),
        q=pltpu.VMEM((micro, rows, heads_width), bf16),
        k=pltpu.VMEM((micro, rows, heads_width), bf16),
        v=pltpu.VMEM((micro, rows, heads_width), bf16),
        o=pltpu.VMEM((micro, rows, heads_width), bf16),
        logsum=pltpu.VMEM((micro, rows, LANES), f32),
        mixer=pltpu.VMEM((LANES, width), f32),
        residual=pltpu.VMEM((LANES, LANES), f32),
        prev_t=pltpu.VMEM((micro, LANES, owned), f32),
        cols=pltpu.VMEM((micro, owned, 16), i32),
        gates=pltpu.VMEM((micro, owned, LANES), f32),
        place_col=pltpu.VMEM((micro, owned, 2), i32),
        place_row=pltpu.VMEM((micro, 2, owned), i32),
        bias=pltpu.VMEM((rows, rows), bf16),
        arrived=pltpu.VMEM((depth, 2, slots, width), bf16),
        part_in=pltpu.VMEM((slots, width), bf16),
        back=pltpu.VMEM((micro, slots, width), bf16),
        half_in=pltpu.VMEM((2, micro, owned, width), bf16),
        hop_in=pltpu.VMEM((min(2, cfg.sections - 1), micro, owned, width), bf16),
        outgoing=pltpu.VMEM((depth, cfg.experts * cfg.main, width), bf16),
        part_out=pltpu.VMEM((slots, width), bf16),
        result=pltpu.VMEM((depth, slots, width), bf16),
        partial=pltpu.VMEM((max(slots, owned), width), f32),
        half_out=pltpu.VMEM((owned, width), bf16),
        hop_out=pltpu.VMEM((depth, owned, width), bf16),
        inside=pltpu.VMEM((depth, 2 * slots, inner), bf16),
        **rem_scratch,
        by_up=pltpu.VMEM((depth, 2 * slots, inner), bf16),
        by_gate=pltpu.VMEM((depth, 2 * slots, inner), bf16),
        dz=pltpu.VMEM((depth, owned, width), f32),
        dh=pltpu.VMEM((owned, width), f32),
        dnorm=pltpu.VMEM((depth, owned, width), f32),
        da=pltpu.VMEM((rows, width), bf16),
        do=pltpu.VMEM((rows, heads_width), bf16),
        dq=pltpu.VMEM((rows, heads_width), bf16),
        dk=pltpu.VMEM((rows, heads_width), bf16),
        dv=pltpu.VMEM((rows, heads_width), bf16),
        mix=pltpu.VMEM((rows, LANES), f32),
        mix_k=pltpu.VMEM((rows, LANES), f32),
        mix_v=pltpu.VMEM((rows, LANES), f32),
        pair_send=dma((8, micro, 3)),
        pair_recv=dma((8, micro, 3)),
        hop_send=dma((2, micro)),
        hop_recv=dma((2, micro)),
        a2a_send=dma((4, micro, cfg.experts)),
        a2a_recv=dma((4, micro, cfg.experts)),
        local=dma((17, micro)),
        keep=dma((2, micro, 4)),
        fetch=dma((3,)),
    )
    names = [*ins, *outs, *hbm_outs, *scratch]
    flops = 2 * micro * (2 * slots * width * inner * 6 + rows * width * heads_width * 10)
    results = pl.pallas_call(
        functools.partial(chain_kernel, cfg, names),
        out_shape=[*outs.values(), *hbm_outs.values()],
        in_specs=[
            smem if name == "lengths" else anywhere if name in far else vmem for name in ins
        ],
        out_specs=[vmem] * len(outs) + [anywhere] * len(hbm_outs),
        scratch_shapes=[*scratch.values()],
        compiler_params=pltpu.CompilerParams(
            collective_id=0, has_side_effects=True, vmem_limit_bytes=60 * 2**20
        ),
        cost_estimate=pl.CostEstimate(flops=flops, bytes_accessed=50_000_000, transcendentals=0),
    )(*ins.values())
    return types.SimpleNamespace(**dict(zip([*outs, *hbm_outs], results, strict=True)))


def tail_kernel(cfg, names, *refs):
    r = types.SimpleNamespace(**dict(zip(names, refs, strict=True)))
    experts, width, pad = cfg.experts, cfg.width, cfg.small_pad
    side = width // 2
    outer = experts // 2
    me, core = lax.axis_index("expert"), lax.axis_index("tensor")
    mine_out, mine_in = me // 2, lax.rem(me, 2)
    beside = me + 1 - 2 * mine_in
    pieces = len(cfg.piece_rows)
    starts = [sum(cfg.piece_rows[:c]) * experts for c in range(pieces)]

    def peer_of(k):
        place = lax.rem(mine_out + k, outer)
        return place, place * 2 + mine_in

    barrier = pltpu.get_barrier_semaphore()
    pl.semaphore_signal(barrier, inc=1, device_id={"tensor": 1 - core}, device_id_type=MESH)
    pl.semaphore_signal(barrier, inc=1, device_id={"expert": beside}, device_id_type=MESH)

    def greet(k, carry):
        pl.semaphore_signal(barrier, inc=1, device_id={"expert": peer_of(k)[1]}, device_id_type=MESH)
        return carry

    lax.fori_loop(1, outer, greet, 0)

    loads = [
        pltpu.make_async_copy(source, target, r.fetch.at[k])
        for k, (source, target) in enumerate(
            (
                (r.h_rows, r.rows_v),
                (r.h_gate, r.gate_v),
                (r.h_up, r.up_v),
                (r.h_grads, r.grads_v),
                (r.h_inside, r.gate_v),
            )
        )
    ]
    for copy in loads[:4]:
        copy.start()

    r.pack[...] = jnp.zeros_like(r.pack)
    r.pack[:pad, :] = r.mixer_grad[:pad, :side]
    r.pack[pad : 2 * pad, :] = r.mixer_grad[:pad, side:]
    r.pack[2 * pad : 2 * pad + 8, :] = r.rows_grad[:, :side]
    r.pack[2 * pad + 8 : 2 * pad + 16, :] = r.rows_grad[:, side:]
    r.pack[2 * pad + 16 : 3 * pad + 16, :LANES] = r.residual_grad[:pad, :]
    r.pack_out[...] = r.pack[...].astype(bf16)
    pl.semaphore_wait(barrier, outer + 1)
    pack_copy = pltpu.make_async_remote_copy(
        src_ref=r.pack_out,
        dst_ref=r.pack_in,
        send_sem=r.pack_sem.at[0],
        recv_sem=r.pack_sem.at[1],
        device_id={"tensor": 1 - core},
        device_id_type=MESH,
    )
    pack_copy.start()

    def span(start, index, size):
        return pl.ds(pl.multiple_of(start + index * size, 16), size)

    def over_x(stage, c, source, target, from_rows, to_rows):
        return pltpu.make_async_remote_copy(
            src_ref=source.at[from_rows],
            dst_ref=target.at[to_rows],
            send_sem=r.x_send.at[stage, c],
            recv_sem=r.x_recv.at[stage, c],
            device_id={"expert": beside},
            device_id_type=MESH,
        )

    def over_z(stage, c, place, landed, peer, source, target):
        return pltpu.make_async_remote_copy(
            src_ref=source,
            dst_ref=target,
            send_sem=r.z_send.at[stage, c, place],
            recv_sem=r.z_recv.at[stage, c, landed],
            device_id={"expert": peer},
            device_id_type=MESH,
        )

    def half_of(c, which):
        return span(starts[c], which, outer * cfg.piece_rows[c])

    def landing(c):
        return pl.ds(starts[c] // 2, outer * cfg.piece_rows[c])

    def scatter_x(c):
        return over_x(0, c, r.sent, r.x_in, half_of(c, 1 - mine_in), landing(c))

    def gather_x(c, which):
        return over_x(1, c, r.summed, r.summed, half_of(c, which), half_of(c, which))

    def scatter_z(c, place, landed, peer):
        size = cfg.piece_rows[c]
        return over_z(
            0,
            c,
            place,
            landed,
            peer,
            r.z_out.at[span(starts[c] // 2, place, size)],
            r.z_in.at[landed, pl.ds(starts[c] // experts, size)],
        )

    def final(c, place):
        return span(starts[c], mine_in * outer + place, cfg.piece_rows[c])

    def gather_z(c, place, landed, peer):
        rows = final(c, landed)
        return over_z(1, c, place, landed, peer, r.summed.at[rows], r.summed.at[rows])

    def weight_grad(left, right):
        return dot_tn(left.reshape(-1, left.shape[-1]), right.reshape(-1, right.shape[-1]))

    products = ((r.h_norm, r.h_dq), (r.h_norm, r.h_dk), (r.h_norm, r.h_dv), (r.h_da, r.h_o))
    for c in range(pieces):
        rows = pl.ds(starts[c], experts * cfg.piece_rows[c])
        if c < 4:
            left, right = products[c]
            value = weight_grad(left[...], right[...])
            if value.shape[0] != experts * cfg.piece_rows[c]:
                r.sent[rows, :] = jnp.zeros((experts * cfg.piece_rows[c], side), bf16)
            r.sent[pl.ds(starts[c], value.shape[0]), :] = value.astype(bf16)
        else:
            pack_copy.wait()
            r.sent[rows, :] = (r.pack[...] + wide(r.pack_in[...])).astype(bf16)
        scatter_x(c).start()

    rows_all = cfg.micro * 2 * cfg.slots
    tile = 256
    steps = []
    for left, right, target in (
        (r.rows_v, r.gate_v, r.gate_grad),
        (r.rows_v, r.up_v, r.up_grad),
        (r.gate_v, r.grads_v, r.down_grad),
    ):
        for t in range(left.shape[-1] // tile):
            needs = ((0, 1), (0, 2), (3, 4))[len(steps) // (width // tile) if target is not r.down_grad else 2]
            steps.append((left, right, target, t, needs))

    loaded = set()
    flying = [None, None]

    def expert_step(index):
        left, right, target, t, needs = steps[index]
        if index == width // tile:
            loads[4].start()
        for k in needs:
            if k not in loaded:
                loads[k].wait()
                loaded.add(k)
        slot = index % 2
        if flying[slot] is not None:
            flying[slot].wait()
        wide_out = right.shape[-1]
        a = left[..., t * tile : (t + 1) * tile].reshape(rows_all, tile)
        r.stage[slot, :, :wide_out] = dot_tn(a, right[...].reshape(rows_all, wide_out)).astype(bf16)
        copy = pltpu.make_async_copy(
            r.stage.at[slot, :, pl.ds(0, wide_out)],
            target.at[pl.ds(t * tile, tile)],
            r.step_sem.at[index],
        )
        copy.start()
        flying[slot] = copy

    done = 0
    for c in range(pieces):
        upto = len(steps) * (c + 1) // pieces
        while done < upto:
            expert_step(done)
            done += 1
        scatter_x(c).wait_recv()
        rows = landing(c)
        r.z_out[rows, :] = (wide(r.sent[half_of(c, mine_in), :]) + wide(r.x_in[rows, :])).astype(bf16)

        def out_z(k, carry, c=c):
            place, peer = peer_of(k)
            scatter_z(c, place, mine_out, peer).start()
            return carry

        lax.fori_loop(1, outer, out_z, 0)

    for c in range(pieces):
        size = cfg.piece_rows[c]

        def add_z(k, total, c=c, size=size):
            place, peer = peer_of(k)
            scatter_z(c, place, place, peer).wait_recv()
            return total + wide(r.z_in[place, pl.ds(starts[c] // experts, size), :])

        total = lax.fori_loop(1, outer, add_z, wide(r.z_out[span(starts[c] // 2, mine_out, size), :]))
        r.summed[final(c, mine_out), :] = total.astype(bf16)

        def back_z(k, carry, c=c):
            place, peer = peer_of(k)
            gather_z(c, place, mine_out, peer).start()
            return carry

        lax.fori_loop(1, outer, back_z, 0)

    for c in range(pieces):

        def wait_z(k, carry, c=c):
            place, peer = peer_of(k)
            gather_z(c, place, place, peer).wait_recv()
            return carry

        lax.fori_loop(1, outer, wait_z, 0)
        gather_x(c, mine_in).start()
    for c in range(pieces):
        gather_x(c, 1 - mine_in).wait_recv()
    for c in range(pieces):
        scatter_x(c).wait_send()
        gather_x(c, mine_in).wait_send()

        def sent_z(k, carry, c=c):
            place, peer = peer_of(k)
            scatter_z(c, place, mine_out, peer).wait_send()
            gather_z(c, place, mine_out, peer).wait_send()
            return carry

        lax.fori_loop(1, outer, sent_z, 0)
    for copy in flying:
        copy.wait()


def run_tail(cfg, got):
    vmem, anywhere = pl.BlockSpec(memory_space=pltpu.VMEM), pl.BlockSpec(memory_space=pl.ANY)
    micro, width, inner, slots, experts = cfg.micro, cfg.width, cfg.inner, cfg.slots, cfg.experts
    side, outer = width // 2, experts // 2
    piece = -(-width // (16 * experts)) * 16
    small = -(-(3 * cfg.small_pad + 16) // (16 * experts)) * 16
    cfg.piece_rows = [piece] * 4 + [small]
    total = sum(cfg.piece_rows) * experts
    near = dict(
        h_norm=got.h_norm,
        h_da=got.h_da,
        h_o=got.h_o,
        h_dq=got.h_dq,
        h_dk=got.h_dk,
        h_dv=got.h_dv,
        mixer_grad=got.mixer_grad,
        residual_grad=got.residual_grad,
        rows_grad=got.rows_grad,
    )
    far = dict(
        h_rows=got.h_rows,
        h_grads=got.h_grads,
        h_inside=got.h_inside,
        h_up=got.h_up,
        h_gate=got.h_gate,
    )
    shape, dma = jax.ShapeDtypeStruct, pltpu.SemaphoreType.DMA
    outs = dict(
        summed=shape((total, side), bf16),
        gate_grad=shape((width, inner), bf16),
        up_grad=shape((width, inner), bf16),
        down_grad=shape((inner, width), bf16),
    )
    scratch = dict(
        rows_v=pltpu.VMEM((micro, 2, slots, width), bf16),
        grads_v=pltpu.VMEM((micro, 2, slots, width), bf16),
        up_v=pltpu.VMEM((micro, 2 * slots, inner), bf16),
        gate_v=pltpu.VMEM((micro, 2 * slots, inner), bf16),
        sent=pltpu.VMEM((total, side), bf16),
        x_in=pltpu.VMEM((total // 2, side), bf16),
        z_out=pltpu.VMEM((total // 2, side), bf16),
        z_in=pltpu.VMEM((outer, total // experts, side), bf16),
        pack=pltpu.VMEM((small * experts, side), f32),
        pack_out=pltpu.VMEM((small * experts, side), bf16),
        pack_in=pltpu.VMEM((small * experts, side), bf16),
        stage=pltpu.VMEM((2, 256, max(inner, width)), bf16),
        fetch=dma((5,)),
        step_sem=dma(((2 * width + inner) // 256,)),
        pack_sem=dma((2,)),
        x_send=dma((2, 5)),
        x_recv=dma((2, 5)),
        z_send=dma((2, 5, outer)),
        z_recv=dma((2, 5, outer)),
    )
    names = [*near, *far, *outs, *scratch]
    results = pl.pallas_call(
        functools.partial(tail_kernel, cfg, names),
        out_shape=[*outs.values()],
        in_specs=[vmem] * len(near) + [anywhere] * len(far),
        out_specs=[vmem] + [anywhere] * 3,
        scratch_shapes=[*scratch.values()],
        compiler_params=pltpu.CompilerParams(
            collective_id=1, has_side_effects=True, vmem_limit_bytes=60 * 2**20
        ),
        cost_estimate=pl.CostEstimate(
            flops=12 * micro * slots * width * inner, bytes_accessed=40_000_000, transcendentals=0
        ),
    )(*near.values(), *far.values())
    return types.SimpleNamespace(
        **dict(zip(outs, results, strict=True)), pad_rows=piece * experts
    )


def rope_tables(rows):
    half_width = HEAD_DIM // 2
    frequency = 10000.0 ** (-2.0 * np.arange(half_width, dtype=np.float64) / HEAD_DIM)
    angles = np.arange(rows, dtype=np.float64)[:, None] * frequency[None, :]
    angles = np.tile(angles, (1, LANES // half_width))
    return np.cos(angles).astype(np.float32), np.sin(angles).astype(np.float32)


def local(
    inputs,
    cotangent,
    prev_logits,
    lengths,
    routes,
    slot_order,
    norm_gain1,
    w_query,
    w_key,
    w_value,
    w_out,
    norm_gain2,
    router,
    router_residual,
    const_gate,
    const_value,
    expert_gate,
    expert_up,
    expert_down,
):
    micro, owned, width = inputs.shape
    tensors, peers = lax.axis_size("tensor"), lax.axis_size("expert")
    choices = router.shape[2]
    experts = choices - 4
    assert experts == peers and tensors == 2
    cap = 9 * 2 * owned // (8 * choices) + 1
    main, rem = cap // 16 * 16, cap % 16
    if rem > 2 or not main:
        main, rem = main + (16 if rem else 0), 0
    rem_rows = -(-rem * peers // 16) * 16
    cfg = types.SimpleNamespace(
        micro=micro,
        owned=owned,
        width=width,
        rows=owned * tensors,
        inner=expert_gate.shape[3],
        heads=w_query.shape[2] // HEAD_DIM,
        experts=experts,
        choices=choices,
        cap=cap,
        main=main,
        rem=rem,
        rem_rows=rem_rows,
        half_rows=peers // 2 * main,
        slots=peers * main + rem_rows,
        depth=micro if peers * main <= 512 else 1,
        sections=lax.axis_size("section"),
        seqs=lengths.shape[2] - 1,
        chunk=owned,
        small_pad=-(-(choices + 2) // 16) * 16,
    )
    cosine, sine = rope_tables(cfg.rows)
    ins = dict(
        lengths=lengths[:, 0],
        inputs=inputs,
        cotangent=cotangent,
        prev_in=jnp.transpose(prev_logits[0], (2, 0, 1)),
        route_row=jnp.swapaxes(routes[0], 1, 2),
        order_row=slot_order[0],
        gain1=norm_gain1,
        gain2=norm_gain2,
        w_query=w_query[0],
        w_key=w_key[0],
        w_value=w_value[0],
        w_out=w_out[0],
        router_in=router[0].T,
        const_gate=const_gate[0],
        residual_in=router_residual[0],
        const_value=const_value[0],
        cosine=jnp.asarray(cosine),
        sine=jnp.asarray(sine),
        gate=expert_gate[0, 0],
        up=expert_up[0, 0],
        down=expert_down[0, 0],
    )
    got = run_chain(cfg, ins)

    tail = run_tail(cfg, got)
    query_grad, key_grad, value_grad, out_grad = (
        wide(tail.summed[c * tail.pad_rows : c * tail.pad_rows + width]) for c in range(4)
    )
    small = wide(tail.summed[4 * tail.pad_rows :])
    pad = cfg.small_pad
    mixer_grad = jnp.concatenate([small[:pad], small[pad : 2 * pad]], axis=1)
    rows_grad = jnp.concatenate([small[2 * pad : 2 * pad + 8], small[2 * pad + 8 : 2 * pad + 16]], axis=1)
    residual_grad = small[2 * pad + 16 : 3 * pad + 16, :LANES]
    return (
        got.layer_out[None],
        got.input_grad[None],
        got.logit_grad[None, :, :, :choices],
        rows_grad[None, 2],
        query_grad[None],
        key_grad[None],
        value_grad[None],
        out_grad.T[None],
        rows_grad[None, 3],
        mixer_grad[:choices].T[None],
        residual_grad[None, :choices, :choices],
        mixer_grad[None, choices : choices + 2],
        rows_grad[None, :2],
        wide(tail.gate_grad)[None, None],
        wide(tail.up_grad)[None, None],
        wide(tail.down_grad)[None, None],
    )


def solution(mesh):
    tokens = ("expert", "tensor")
    in_specs = (
        P(None, tokens, None),
        P(None, tokens, None),
        P("section", None, tokens, None),
        P(None, "expert", None),
        P("section", None, tokens, None),
        P("section", None, tokens, None),
        P("section", None),
        P("section", None, "tensor"),
        P("section", None, "tensor"),
        P("section", None, "tensor"),
        P("section", "tensor", None),
        P("section", None),
        P("section", None, None),
        P("section", None, None),
        P("section", None, None),
        P("section", None, None),
        P("section", "expert", None, "tensor"),
        P("section", "expert", None, "tensor"),
        P("section", "expert", "tensor", None),
    )
    out_specs = (
        P("section", None, tokens, None),
        P("section", None, tokens, None),
        P("section", None, tokens, None),
        P("section", None),
        P("section", None, "tensor"),
        P("section", None, "tensor"),
        P("section", None, "tensor"),
        P("section", "tensor", None),
        P("section", None),
        P("section", None, None),
        P("section", None, None),
        P("section", None, None),
        P("section", None, None),
        P("section", "expert", None, "tensor"),
        P("section", "expert", None, "tensor"),
        P("section", "expert", "tensor", None),
    )
    return jax.shard_map(local, mesh=mesh, in_specs=in_specs, out_specs=out_specs, check_vma=False)
```

profile of v0, /device:TPU:10, one launch (start us, length us, event | category | flops | bytes accessed | tf_op | source)
XLA Modules:
  0.0 406.9 jit_solution(9821590743579335427)
XLA Ops:
  0.6 1.3 copy.46
  1.9 1.4 copy.45
  3.3 294.9 %shard_map.324 = (f32[2,256,128]{2,1,0:T(8,128)}, f32[128,768]{1,0:T(8,128)}, f32[128,128]{1,0:T(8,128)}, f32[8,768]{1,0:T(8,128)}, f32[2,256,768]{2,1,0:T(8,128...) custom-call(s32[2,4]{1,0:T(2,128)} %bitcast.77, ...), custom_call_target="tpu_custom_call" | custom-call | flops 21139292160 | bytes 50000000 | tf_op jit(solution)/shard_map/pallas_call | solution.py:942
  298.3 1.0 slice_bitcast_fusion
  299.2 0.7 copy.37
  300.0 88.5 %shard_map.325 = (bf16[3200,384]{1,0:T(8,128)(2,1)}, bf16[768,1024]{1,0:T(8,128)(2,1)}, bf16[768,1024]{1,0:T(8,128)(2,1)}, bf16[1024,768]{1,0:T(8,128)(2,1)}) custom-call(bf16[2,512,768]{2,1,0:T(8,128)(2,1)} %get-tuple-element.40.refs_0_, bf16[2,512,768]{2,1,0:T(8,128)(2,1)} %get-tuple-element.41.refs_1_, bf16[2,512,384]{2,1,0:T(8,128)(2,1)} %get-tuple-element.42.refs_2_, ...), custom_call_target="tpu_custom_call" | custom-call | flops 7549747200 | bytes 40000000 | tf_op jit(solution)/shard_map/pallas_call | solution.py:1240
  388.4 0.9 slice_convert_fusion
  389.3 0.6 copy.40
  390.0 0.6 pad_maximum_fusion.2
  390.5 0.6 fusion
  391.2 0.7 copy.39
  391.8 3.5 convert_bitcast_fusion
  395.3 0.0 copy-start.4
  395.3 1.4 copy.38
  396.7 0.2 copy-done.4
  396.9 0.0 copy-start
  396.9 0.0 copy-start.1
  396.9 1.9 bitcast_convert_fusion
  398.8 0.1 copy-done
  398.8 1.1 copy-done.1
  399.9 0.0 copy-start.3
  399.9 3.4 bitcast_convert_fusion.1
  403.4 0.0 copy-done.3
  403.4 0.0 copy-start.2
  403.4 1.1 copy.49
  404.5 0.8 copy-done.2
  405.3 1.1 copy.50
  (4 shorter events, 0.0 us)
Async XLA Ops:
  395.3 1.6 copy-start.4
  396.9 2.0 copy-start
  396.9 3.0 copy-start.1
  399.9 3.5 copy-start.3
  403.4 2.0 copy-start.2
where the time goes:
time: 415 us; the launch traced here: 407 us
  Pallas kernels  383 us (92%)
  local copies, waits for them, and re-layouts  11.5 us (3%)
  other arithmetic  10.9 us (3%)
    pallas_call x1, Pallas kernels, run_chain(): pl.pallas_call(functools.partial(chain_kernel, cfg, names), out_shape=[*o...  295 us
    pallas_call x1, Pallas kernels, run_tail(): pl.pallas_call(functools.partial(tail_kernel, cfg, names), out_shape=[*ou...  88.5 us
    unnamed x18, local copies, waits for them, and re-layouts  10.5 us

commit v1 on v0

--- a/solution.py
+++ b/solution.py
@@ -179,6 +179,62 @@
             device_id_type=MESH,
         )
 
+    outer = experts // 2
+    mirrored = outer - 1 - me // 2
+
+    def to_relay(kind, m, peer, source):
+        place = lax.rem(peer, 2)
+        return pltpu.make_async_remote_copy(
+            src_ref=source.at[slot_rows(peer)],
+            dst_ref=r.relay.at[kind, m, place],
+            send_sem=r.a2a_send.at[kind, m, peer],
+            recv_sem=r.relay_recv.at[kind, m, place],
+            device_id={"section": 1 - sec},
+            device_id_type=MESH,
+        )
+
+    def relay_copy(kind, m, place):
+        target = (r.arrived.at[m, core], r.back.at[m], r.arrived.at[m, core], grad_back(m))[kind]
+        return pltpu.make_async_remote_copy(
+            src_ref=r.relay.at[kind, m, place],
+            dst_ref=target.at[slot_rows(me)],
+            send_sem=r.relay_send.at[kind, m, place],
+            recv_sem=r.a2a_recv.at[kind, m, me],
+            device_id={"section": 1 - sec, "expert": mirrored * 2 + place},
+            device_id_type=MESH,
+        )
+
+    def relay(kind, m):
+        for place in range(2):
+            pltpu.make_async_remote_copy(
+                src_ref=r.relay.at[kind, m, place],
+                dst_ref=r.relay.at[kind, m, place],
+                send_sem=r.relay_send.at[kind, m, place],
+                recv_sem=r.relay_recv.at[kind, m, place],
+                device_id={"section": 1 - sec},
+                device_id_type=MESH,
+            ).wait_recv()
+            relay_copy(kind, m, place).start()
+
+    def relays_for_first():
+        return [(k, m) for k in range(2) for m in range(micro) if (k, m) != (1, micro - 1)]
+
+    def send_block(kind, m, peer, source, target):
+        if not cfg.relay:
+            exchange(kind, m, peer, me, source, target).start()
+            return
+        aside = peer // 2 == mirrored
+        if kind == 1:
+            aside = aside & ((sec > 0) | (m < micro - 1))
+
+        @pl.when(aside)
+        def _():
+            to_relay(kind, m, peer, source).start()
+
+        @pl.when(jnp.logical_not(aside))
+        def _():
+            exchange(kind, m, peer, me, source, target).start()
+
     def lay_rem(ref, value):
         for k in range(rem):
             ref[:, k, :] = value[k * experts : (k + 1) * experts]
@@ -195,7 +251,7 @@
         outgoing, mine = r.outgoing.at[d], r.arrived.at[d, core]
         r.outgoing[d] = value[:rem_start].astype(bf16)
         for g in (1, 0):
-            peers_in(g, lambda p: exchange(kind, m, p, me, outgoing, mine).start())
+            peers_in(g, lambda p: send_block(kind, m, p, outgoing, mine))
         if rem:
             rem_out, rem_in = r.rem_out.at[d], r.rem_in.at[d]
             lay_rem(rem_out, value[rem_start:])
@@ -254,8 +310,16 @@
     ]
     for copy in weights:
         copy.start()
+    if cfg.relay:
+        for place in range(2):
+            pl.semaphore_signal(
+                barrier,
+                inc=1,
+                device_id={"section": 1 - sec, "expert": mirrored * 2 + place},
+                device_id_type=MESH,
+            )
     beside = (sec > 0).astype(i32) + (sec < sections - 1).astype(i32)
-    pl.semaphore_wait(barrier, experts + beside)
+    pl.semaphore_wait(barrier, experts + beside + (2 if cfg.relay else 0))
 
     r.mixer[...] = jnp.zeros_like(r.mixer)
     r.mixer[:choices, :] = r.router_in[...]
@@ -391,7 +455,7 @@
             for copy in forward_pair(g, core, mine):
                 copy.wait_send()
             put(result, g, value.astype(bf16))
-            peers_in(g, lambda p: exchange(kind + 1, m, p, me, result, target).start())
+            peers_in(g, lambda p: send_block(kind + 1, m, p, result, target))
             if g == 1 and rem:
                 lay_rem(rem_result, value[half_rows:])
                 for which in (1, 0):
@@ -817,12 +881,44 @@
             def _():
                 grad_start(m)
 
+        every = [(k, m) for k in range(4) for m in range(micro)]
+        if cfg.relay:
+
+            @pl.when(is_last)
+            def _():
+                for k, m in relays_for_first():
+                    relay(k, m)
+
         all_of(attend, attend_send)
         all_of(experts_forward)
         all_of(turn)
+        if cfg.relay:
+
+            @pl.when(is_first)
+            def _():
+                for k, m in every:
+                    relay(k, m)
+
         all_of(start_rest)
         all_of(experts_backward)
         all_of(grad_attend, grad_finish)
+        if cfg.relay:
+
+            @pl.when(is_last)
+            def _():
+                for k, m in every:
+                    if k >= 2:
+                        relay(k, m)
+                for k, m in relays_for_first() + [(k, m) for k, m in every if k >= 2]:
+                    for place in range(2):
+                        relay_copy(k, m, place).wait_send()
+
+            @pl.when(is_first)
+            def _():
+                for k, m in every:
+                    for place in range(2):
+                        relay_copy(k, m, place).wait_send()
+
         for m in range(micro):
             settle_backward(m)
     else:
@@ -879,6 +975,13 @@
         rem_sem = dma((4, micro, cfg.experts))
         rem_scratch |= dict(
             rem_out=last, rem_in=last, rem_result=last, rem_back=last, rem_send=rem_sem, rem_recv=rem_sem
+        )
+    if cfg.relay:
+        relay_sem = dma((4, micro, 2))
+        rem_scratch |= dict(
+            relay=pltpu.VMEM((4, micro, 2, cfg.main, width), bf16),
+            relay_send=relay_sem,
+            relay_recv=relay_sem,
         )
     scratch = dict(
         gate_v=pltpu.VMEM((width, inner), bf16),
@@ -1315,6 +1418,7 @@
         chunk=owned,
         small_pad=-(-(choices + 2) // 16) * 16,
     )
+    cfg.relay = cfg.depth == micro and cfg.sections == 2 and peers == 8
     cosine, sine = rope_tables(cfg.rows)
     ins = dict(
         lengths=lengths[:, 0],

time: 415 us -> 379 us (0.913); the launches traced: 407 us -> 383 us
  Pallas kernels: 383 us -> 359 us
    pallas_call x1, Pallas kernels: 295 us -> 275 us  [run_chain(): pl.pallas_call(functools.partial(chain_kernel, cfg, names), out_shape=[*o...]
    pallas_call x1, Pallas kernels: 88.5 us -> 84.2 us  [run_tail(): pl.pallas_call(functools.partial(tail_kernel, cfg, names), out_shape=[*ou...]
where the time goes in v1:
time: 379 us; the launch traced here: 383 us
  Pallas kernels  359 us (95%)
  local copies, waits for them, and re-layouts  11.5 us (3%)
  other arithmetic  10.9 us (3%)
    pallas_call x1, Pallas kernels, run_chain(): pl.pallas_call(functools.partial(chain_kernel, cfg, names), out_shape=[*o...  275 us
    pallas_call x1, Pallas kernels, run_tail(): pl.pallas_call(functools.partial(tail_kernel, cfg, names), out_shape=[*ou...  84.2 us
    unnamed x18, local copies, waits for them, and re-layouts  10.5 us

profile of v1, /device:TPU:10, one launch (start us, length us, event | category | flops | bytes accessed | tf_op | source)
XLA Modules:
  0.0 382.8 jit_solution(8422849876380125068)
XLA Ops:
  0.6 1.3 copy.46
  1.9 1.4 copy.45
  3.3 275.3 %shard_map.324 = (f32[2,256,128]{2,1,0:T(8,128)}, f32[128,768]{1,0:T(8,128)}, f32[128,128]{1,0:T(8,128)}, f32[8,768]{1,0:T(8,128)}, f32[2,256,768]{2,1,0:T(8,128...) custom-call(s32[2,4]{1,0:T(2,128)} %bitcast.77, ...), custom_call_target="tpu_custom_call" | custom-call | flops 21139292160 | bytes 50000000 | tf_op jit(solution)/shard_map/pallas_call | solution.py:1045
  278.6 1.0 slice_bitcast_fusion
  279.6 0.7 copy.37
  280.3 84.2 %shard_map.325 = (bf16[3200,384]{1,0:T(8,128)(2,1)}, bf16[768,1024]{1,0:T(8,128)(2,1)}, bf16[768,1024]{1,0:T(8,128)(2,1)}, bf16[1024,768]{1,0:T(8,128)(2,1)}) custom-call(bf16[2,512,768]{2,1,0:T(8,128)(2,1)} %get-tuple-element.40.refs_0_, bf16[2,512,768]{2,1,0:T(8,128)(2,1)} %get-tuple-element.41.refs_1_, bf16[2,512,384]{2,1,0:T(8,128)(2,1)} %get-tuple-element.42.refs_2_, ...), custom_call_target="tpu_custom_call" | custom-call | flops 7549747200 | bytes 40000000 | tf_op jit(solution)/shard_map/pallas_call | solution.py:1343
  364.5 0.9 slice_convert_fusion
  365.4 0.6 copy.40
  366.0 0.6 pad_maximum_fusion.2
  366.6 0.6 fusion
  367.2 0.7 copy.39
  367.9 3.5 convert_bitcast_fusion
  371.4 0.0 copy-start.4
  371.4 1.4 copy.38
  372.7 0.2 copy-done.4
  373.0 0.0 copy-start
  373.0 0.0 copy-start.1
  373.0 1.9 bitcast_convert_fusion
  374.9 0.1 copy-done
  374.9 1.1 copy-done.1
  376.0 0.0 copy-start.3
  376.0 3.4 bitcast_convert_fusion.1
  379.4 0.0 copy-done.3
  379.4 0.0 copy-start.2
  379.4 1.1 copy.49
  380.6 0.8 copy-done.2
  381.4 1.1 copy.50
  (4 shorter events, 0.0 us)
Async XLA Ops:
  371.4 1.6 copy-start.4
  373.0 2.0 copy-start
  373.0 3.0 copy-start.1
  376.0 3.5 copy-start.3
  379.4 2.0 copy-start.2

commit v2 on v1

--- a/solution.py
+++ b/solution.py
@@ -346,7 +346,7 @@
             piece = slice(c * chunk, (c + 1) * chunk)
             key = iota((chunk, rows), 1)
             seen = (key <= row[piece]) & (key >= start[piece])
-            r.bias[piece, :] = jnp.where(seen, 0.0, -1e30).astype(bf16)
+            r.bias[piece, :] = jnp.where(seen, 0.0, -1e30).astype(r.bias.dtype)
 
     def routing(m):
         lane = iota((owned, LANES), 1)
@@ -513,8 +513,8 @@
         def project(some):
             normed = r.norm[m, some, :]
             cosine, sine = r.cosine[some, :], r.sine[some, :]
-            for stash, weight in ((r.q, r.w_query), (r.k, r.w_key)):
-                flat = dot(normed, weight[...])
+            for stash, weight, factor in ((r.q, r.w_query, scale), (r.k, r.w_key, 1.0)):
+                flat = dot(normed, weight[...]) * factor
                 for p in range(pairs):
                     lanes = slice(p * LANES, (p + 1) * LANES)
                     stash[m, some, lanes] = turned(flat[:, lanes], cosine, sine).astype(bf16)
@@ -536,12 +536,11 @@
                 km, vm = k2 * keep, v2 * keep
                 for c in range(rows // chunk):
                     piece, reach = slice(c * chunk, (c + 1) * chunk), (c + 1) * chunk
-                    scores = dot_nt(q2[piece], km[:reach]) * scale + wide(r.bias[piece, :reach])
+                    scores = dot_nt(q2[piece], km[:reach]) + wide(r.bias[piece, :reach])
                     peak = jnp.max(scores, axis=-1, keepdims=True)
                     shifted = jnp.exp(scores - peak)
                     total = jnp.sum(shifted, axis=-1, keepdims=True)
-                    probs = (shifted * (1.0 / total)).astype(bf16)
-                    mixed = dot(probs, vm[:reach])
+                    mixed = dot(shifted.astype(bf16), vm[:reach]) * (1.0 / total)
                     if half == 0:
                         r.mix[piece, :] = mixed
                     else:
@@ -782,7 +781,7 @@
                 km, vm, qm, dom = k2 * keep, v2 * keep, q2 * keep, do2 * keep
                 for c in range(rows // chunk):
                     piece, reach = slice(c * chunk, (c + 1) * chunk), (c + 1) * chunk
-                    scores = dot_nt(q2[piece], km[:reach]) * scale + wide(r.bias[piece, :reach])
+                    scores = dot_nt(q2[piece], km[:reach]) + wide(r.bias[piece, :reach])
                     total = jnp.sum(
                         jnp.where(head_lane == 2 * p + half, r.logsum[m, piece, :], 0.0),
                         axis=1,
@@ -805,7 +804,7 @@
                     r.mix_k[:reach, :] += dk
                     r.mix_v[:reach, :] += dv
             r.dq[:, lanes] = (turned_back(r.mix[...], r.cosine[...], r.sine[...]) * scale).astype(bf16)
-            r.dk[:, lanes] = (turned_back(r.mix_k[...], r.cosine[...], r.sine[...]) * scale).astype(bf16)
+            r.dk[:, lanes] = turned_back(r.mix_k[...], r.cosine[...], r.sine[...]).astype(bf16)
             r.dv[:, lanes] = r.mix_v[...].astype(bf16)
             return inner
 
@@ -1003,7 +1002,7 @@
         gates=pltpu.VMEM((micro, owned, LANES), f32),
         place_col=pltpu.VMEM((micro, owned, 2), i32),
         place_row=pltpu.VMEM((micro, 2, owned), i32),
-        bias=pltpu.VMEM((rows, rows), bf16),
+        bias=pltpu.VMEM((rows, rows), f32 if depth == micro else bf16),
         arrived=pltpu.VMEM((depth, 2, slots, width), bf16),
         part_in=pltpu.VMEM((slots, width), bf16),
         back=pltpu.VMEM((micro, slots, width), bf16),
@@ -1173,18 +1172,21 @@
     def weight_grad(left, right):
         return dot_tn(left.reshape(-1, left.shape[-1]), right.reshape(-1, right.shape[-1]))
 
-    products = ((r.h_norm, r.h_dq), (r.h_norm, r.h_dk), (r.h_norm, r.h_dv), (r.h_da, r.h_o))
-    for c in range(pieces):
+    products = ((r.h_da, r.h_o), (r.h_norm, r.h_dv), (r.h_norm, r.h_dk), (r.h_norm, r.h_dq))
+    splits = cfg.splits
+
+    def launch(c):
         rows = pl.ds(starts[c], experts * cfg.piece_rows[c])
-        if c < 4:
-            left, right = products[c]
-            value = weight_grad(left[...], right[...])
-            if value.shape[0] != experts * cfg.piece_rows[c]:
-                r.sent[rows, :] = jnp.zeros((experts * cfg.piece_rows[c], side), bf16)
-            r.sent[pl.ds(starts[c], value.shape[0]), :] = value.astype(bf16)
-        else:
+        if c == pieces - 1:
             pack_copy.wait()
             r.sent[rows, :] = (r.pack[...] + wide(r.pack_in[...])).astype(bf16)
+        elif c % splits == 0:
+            left, right = products[c // splits]
+            value = weight_grad(left[...], right[...])
+            covered = splits * experts * cfg.piece_rows[c]
+            if value.shape[0] != covered:
+                r.sent[pl.ds(starts[c], covered), :] = jnp.zeros((covered, side), bf16)
+            r.sent[pl.ds(starts[c], value.shape[0]), :] = value.astype(bf16)
         scatter_x(c).start()
 
     rows_all = cfg.micro * 2 * cfg.slots
@@ -1224,27 +1226,22 @@
         copy.start()
         flying[slot] = copy
 
-    done = 0
-    for c in range(pieces):
-        upto = len(steps) * (c + 1) // pieces
-        while done < upto:
-            expert_step(done)
-            done += 1
+    def reduce_x(c):
         scatter_x(c).wait_recv()
         rows = landing(c)
         r.z_out[rows, :] = (wide(r.sent[half_of(c, mine_in), :]) + wide(r.x_in[rows, :])).astype(bf16)
 
-        def out_z(k, carry, c=c):
+        def out_z(k, carry):
             place, peer = peer_of(k)
             scatter_z(c, place, mine_out, peer).start()
             return carry
 
         lax.fori_loop(1, outer, out_z, 0)
 
-    for c in range(pieces):
+    def reduce_z(c):
         size = cfg.piece_rows[c]
 
-        def add_z(k, total, c=c, size=size):
+        def add_z(k, total):
             place, peer = peer_of(k)
             scatter_z(c, place, place, peer).wait_recv()
             return total + wide(r.z_in[place, pl.ds(starts[c] // experts, size), :])
@@ -1252,22 +1249,37 @@
         total = lax.fori_loop(1, outer, add_z, wide(r.z_out[span(starts[c] // 2, mine_out, size), :]))
         r.summed[final(c, mine_out), :] = total.astype(bf16)
 
-        def back_z(k, carry, c=c):
+        def back_z(k, carry):
             place, peer = peer_of(k)
             gather_z(c, place, mine_out, peer).start()
             return carry
 
         lax.fori_loop(1, outer, back_z, 0)
 
-    for c in range(pieces):
-
-        def wait_z(k, carry, c=c):
+    def spread_x(c):
+        def wait_z(k, carry):
             place, peer = peer_of(k)
             gather_z(c, place, place, peer).wait_recv()
             return carry
 
         lax.fori_loop(1, outer, wait_z, 0)
         gather_x(c, mine_in).start()
+
+    done = 0
+    launch(0)
+    launch(1)
+    for k in range(pieces + 4):
+        if k < pieces:
+            reduce_x(k)
+        if k + 2 < pieces:
+            launch(k + 2)
+        if 0 <= k - 2 < pieces:
+            reduce_z(k - 2)
+        if 0 <= k - 4 < pieces:
+            spread_x(k - 4)
+        while done < min(len(steps), len(steps) * (k + 1) // pieces):
+            expert_step(done)
+            done += 1
     for c in range(pieces):
         gather_x(c, 1 - mine_in).wait_recv()
     for c in range(pieces):
@@ -1289,9 +1301,10 @@
     vmem, anywhere = pl.BlockSpec(memory_space=pltpu.VMEM), pl.BlockSpec(memory_space=pl.ANY)
     micro, width, inner, slots, experts = cfg.micro, cfg.width, cfg.inner, cfg.slots, cfg.experts
     side, outer = width // 2, experts // 2
-    piece = -(-width // (16 * experts)) * 16
+    cfg.splits = 2 if width % (32 * experts) == 0 else 1
+    piece = -(-width // (16 * cfg.splits * experts)) * 16
     small = -(-(3 * cfg.small_pad + 16) // (16 * experts)) * 16
-    cfg.piece_rows = [piece] * 4 + [small]
+    cfg.piece_rows = [piece] * (4 * cfg.splits) + [small]
     total = sum(cfg.piece_rows) * experts
     near = dict(
         h_norm=got.h_norm,
@@ -1334,10 +1347,10 @@
         fetch=dma((5,)),
         step_sem=dma(((2 * width + inner) // 256,)),
         pack_sem=dma((2,)),
-        x_send=dma((2, 5)),
-        x_recv=dma((2, 5)),
-        z_send=dma((2, 5, outer)),
-        z_recv=dma((2, 5, outer)),
+        x_send=dma((2, len(cfg.piece_rows))),
+        x_recv=dma((2, len(cfg.piece_rows))),
+        z_send=dma((2, len(cfg.piece_rows), outer)),
+        z_recv=dma((2, len(cfg.piece_rows), outer)),
     )
     names = [*near, *far, *outs, *scratch]
     results = pl.pallas_call(
@@ -1354,7 +1367,7 @@
         ),
     )(*near.values(), *far.values())
     return types.SimpleNamespace(
-        **dict(zip(outs, results, strict=True)), pad_rows=piece * experts
+        **dict(zip(outs, results, strict=True)), pad_rows=piece * cfg.splits * experts
     )
 
 
@@ -1446,7 +1459,7 @@
     got = run_chain(cfg, ins)
 
     tail = run_tail(cfg, got)
-    query_grad, key_grad, value_grad, out_grad = (
+    out_grad, value_grad, key_grad, query_grad = (
         wide(tail.summed[c * tail.pad_rows : c * tail.pad_rows + width]) for c in range(4)
     )
     small = wide(tail.summed[4 * tail.pad_rows :])

time: 379 us -> 364 us (0.960)
  Pallas kernels: 359 us -> 346 us
    pallas_call x1, Pallas kernels: 84.2 us -> 74.5 us  [run_tail(): pl.pallas_call(functools.partial(tail_kernel, cfg, names), out_shape=[*ou...]
    pallas_call x1, Pallas kernels: 275 us -> 271 us  [run_chain(): pl.pallas_call(functools.partial(chain_kernel, cfg, names), out_shape=[*o...]
where the time goes in v2:
time: 364 us; the launch traced here: 369 us
  Pallas kernels  346 us (95%)
  local copies, waits for them, and re-layouts  11.5 us (3%)
  other arithmetic  10.9 us (3%)
    pallas_call x1, Pallas kernels, run_chain(): pl.pallas_call(functools.partial(chain_kernel, cfg, names), out_shape=[*o...  271 us
    pallas_call x1, Pallas kernels, run_tail(): pl.pallas_call(functools.partial(tail_kernel, cfg, names), out_shape=[*ou...  74.5 us
    unnamed x18, local copies, waits for them, and re-layouts  10.5 us

profile of v2, /device:TPU:10, one launch (start us, length us, event | category | flops | bytes accessed | tf_op | source)
XLA Modules:
  0.0 369.3 jit_solution(3082284115920718993)
XLA Ops:
  0.6 1.3 copy.46
  1.9 1.4 copy.45
  3.3 271.5 %shard_map.324 = (f32[2,256,128]{2,1,0:T(8,128)}, f32[128,768]{1,0:T(8,128)}, f32[128,128]{1,0:T(8,128)}, f32[8,768]{1,0:T(8,128)}, f32[2,256,768]{2,1,0:T(8,128...) custom-call(s32[2,4]{1,0:T(2,128)} %bitcast.77, ...), custom_call_target="tpu_custom_call" | custom-call | flops 21139292160 | bytes 50000000 | tf_op jit(solution)/shard_map/pallas_call | solution.py:1044
  274.8 1.0 slice_bitcast_fusion
  275.8 0.7 copy.37
  276.5 74.5 %shard_map.325 = (bf16[3200,384]{1,0:T(8,128)(2,1)}, bf16[768,1024]{1,0:T(8,128)(2,1)}, bf16[768,1024]{1,0:T(8,128)(2,1)}, bf16[1024,768]{1,0:T(8,128)(2,1)}) custom-call(bf16[2,512,768]{2,1,0:T(8,128)(2,1)} %get-tuple-element.40.refs_0_, bf16[2,512,768]{2,1,0:T(8,128)(2,1)} %get-tuple-element.41.refs_1_, bf16[2,512,384]{2,1,0:T(8,128)(2,1)} %get-tuple-element.42.refs_2_, ...), custom_call_target="tpu_custom_call" | custom-call | flops 7549747200 | bytes 40000000 | tf_op jit(solution)/shard_map/pallas_call | solution.py:1356
  351.0 0.9 slice_convert_fusion
  351.9 0.6 copy.40
  352.6 0.6 pad_maximum_fusion.2
  353.1 0.6 fusion
  353.7 0.7 copy.39
  354.4 3.5 convert_bitcast_fusion
  357.9 0.0 copy-start.4
  357.9 1.4 copy.38
  359.3 0.2 copy-done.4
  359.5 0.0 copy-start
  359.5 0.0 copy-start.1
  359.5 1.9 bitcast_convert_fusion
  361.4 0.1 copy-done
  361.4 1.1 copy-done.1
  362.5 0.0 copy-start.3
  362.5 3.4 bitcast_convert_fusion.1
  366.0 0.0 copy-done.3
  366.0 0.0 copy-start.2
  366.0 1.1 copy.49
  367.1 0.8 copy-done.2
  367.9 1.1 copy.50
  (4 shorter events, 0.0 us)
Async XLA Ops:
  357.9 1.6 copy-start.4
  359.5 2.0 copy-start
  359.5 3.0 copy-start.1
  362.5 3.5 copy-start.3
  366.0 2.0 copy-start.2
